TPU v7x, 32 devices: a whole 2x2x4 slice. The times are simulated.
32 devices in a mesh: day: 16 (over z, y, x), tile: 2 (over core).
Axes of the slice: x: 2, y: 2, z: 4, core: 2. Of those that a mesh axis runs over, the one named last changes fastest.
Arguments:
- library: bfloat16 [512, 2, 16384], P('day', 'tile'), may hold values from 0.05 to 24, as said below
- analog_owner: int32 [64, 30], P('day'), may hold values from 0 to 15, as said below
- analog_offset: int32 [64, 30], P('day'), may hold values from 0 to 31
- picks: int32 [64, 10, 2, 16384], P('day', None, 'tile'), may hold values from 0 to 29
- weights: bfloat16 [64, 10, 2, 16384], P('day', None, 'tile'), may hold values from 0.19921875 to 5
- target_mean: float32 [64], P('day'), may hold values from 0.5 to 5
- ranks: int32 [64, 2, 16384], P('day', 'tile'), may hold values from 0 to 99
- obs_quant: float32 [2, 100, 16384], P('tile', None, 'day'), may hold values from 0.3 to 3
- hist_quant: float32 [2, 100, 16384], P('tile', None, 'day'), may hold values from 0.5 to 2
Outputs:
- corrected: float32 [2, 64, 16384], P('tile', None, 'day')
Inputs may be any that keep to these rules, and one draw needn't show every extreme that they name: `analog_owner`: among the 4 target days of one index of day (aligned blocks of rows), no owner appears more than 15 times, and in every block some owner appears exactly 15 times. `library`: Positive.
All inputs are finite; a program needn't handle non-finite values.
Results may differ from a plain program's by a relative error of at most 0.0003.
Values may be sent and summed in bfloat16 or wider, within the bound.
A program may use at most 128 MiB of HBM per device.

v0:
```python
import jax
import jax.numpy as jnp
from jax import lax
from jax.sharding import PartitionSpec as P


def slot_ranks(owners):
    count = owners.shape[-1]
    same = owners[..., :, None] == owners[..., None, :]
    earlier = jnp.arange(count)[:, None] > jnp.arange(count)[None, :]
    return jnp.sum(same & earlier, axis=-1)


def lookup_rows(table, index_rows):
    levels = jnp.arange(table.shape[-2], dtype=jnp.int32)
    hits = index_rows[:, None, :] == levels[None, :, None]
    return jnp.sum(jnp.where(hits, table, 0.0), axis=1)


def per_device(
    library, analog_owner, analog_offset, picks, weights, target_mean, ranks, obs_quant, hist_quant
):
    blocks = lax.axis_size("day")
    target_days = analog_owner.shape[0]
    row_count = target_days * analog_owner.shape[1]
    capacity = max(2, (2 * row_count + blocks - 1) // blocks)
    own_flat = analog_owner.reshape(row_count)
    offset_flat = analog_offset.reshape(row_count)
    slot_code = own_flat * capacity + slot_ranks(own_flat)
    matches = slot_code[:, None] == jnp.arange(blocks * capacity, dtype=jnp.int32)[None, :]
    table = jnp.sum(jnp.where(matches, offset_flat[:, None], 0), axis=0)
    asked = lax.all_to_all(
        table.reshape(blocks, capacity), "day", split_axis=0, concat_axis=0, tiled=True
    )
    cell_count = library.shape[2]
    outgoing = library[:, 0, :][asked]
    incoming = lax.all_to_all(outgoing, "day", split_axis=0, concat_axis=0, tiled=True)
    received = incoming.reshape(blocks * capacity, cell_count)
    fields = (
        received[slot_code]
        .reshape(target_days, analog_owner.shape[1], cell_count)
        .astype(jnp.float32)
    )
    running = jnp.zeros((target_days, cell_count), jnp.float32)
    weight_sum = jnp.zeros((target_days, cell_count), jnp.float32)
    for which in range(picks.shape[1]):
        chosen = lookup_rows(fields, picks[:, which, 0, :])
        weight_row = weights[:, which, 0, :].astype(jnp.float32)
        running = running + weight_row * chosen
        weight_sum = weight_sum + weight_row
    combined = running / weight_sum
    total = lax.psum(jnp.sum(combined, axis=1), "tile")
    slab_cells = cell_count * lax.axis_size("tile")
    value = combined * (target_mean * slab_cells / total)[:, None]
    local_ratio = obs_quant[0] / hist_quant[0]
    ratio = lax.all_gather(local_ratio, "day", axis=1, tiled=True)
    factor = lookup_rows(ratio[None], ranks[:, 0, :])
    result = lax.all_to_all(value * factor, "day", split_axis=1, concat_axis=0, tiled=True)
    return result[None]


def solution(mesh):
    return jax.shard_map(
        per_device,
        mesh=mesh,
        in_specs=(
            P("day", "tile", None),
            P("day", None),
            P("day", None),
            P("day", None, "tile", None),
            P("day", None, "tile", None),
            P("day"),
            P("day", "tile", None),
            P("tile", None, "day"),
            P("tile", None, "day"),
        ),
        out_specs=P("tile", None, "day"),
        check_vma=False,
    )
```

profile of v0, /device:TPU:25, one launch (start us, length us, event | category | flops | bytes accessed | tf_op | source)
XLA Modules:
  0.0 400.0 jit_solution(18218376728589332268)
XLA Ops:
  6.5 0.9 reshape.160
  9.1 6.4 %all-to-all-start = ((s32[16,1,15]{2,1,0:T(1,128)}), s32[16,1,15]{2,1,0:T(1,128)S(1)}, u32[]{:S(2)}, u32[]{:S(2)}) async-start(s32[16,1,15]{2,1,0:T(1,128)} %bitcast.2), calls=%async_computation | async-start | bytes 16384 | tf_op jit(solution)/shard_map/all_to_all | solution.py:32
  15.6 2.3 div.18
  17.9 2.6 fusion.13
  20.6 1.2 copy_bitcast_fusion.2
  21.7 1.1 copy_bitcast_fusion.4
  23.0 8.6 %gather_fusion = bf16[240,16384]{1,0:T(8,128)(2,1)} fusion(bf16[32,16384]{1,0:T(8,128)(2,1)S(1)} %bitcast.165, s32[1024]{0:T(1024)S(1)} %pad_clamp_fusion.1), kind=kCustom, calls=%fused_computation | custom fusion | bytes 15729600 | tf_op jit(solution)/shard_map/gather | solution.py:36
  31.6 6.9 %reshape.184 = bf16[16,15,16384]{2,1,0:T(8,128)(2,1)} reshape(bf16[240,16384]{1,0:T(8,128)(2,1)} %gather_fusion) | data formatting | bytes 15728640 | tf_op jit(solution)/shard_map/gather | solution.py:36
  38.5 6.5 %all-to-all-start.1 = ((bf16[16,15,16384]{2,1,0:T(8,128)(2,1)}), bf16[16,15,16384]{2,1,0:T(8,128)(2,1)}, u32[]{:S(2)}, u32[]{:S(2)}) async-start(bf16[16,15,16384]{2,1,0:T(8,128)(2,1)} %reshape.184), calls=%async_computation.1 | async-start | bytes 16777216 | tf_op jit(solution)/shard_map/all_to_all | solution.py:37
  45.0 1.2 copy_bitcast_fusion.6
  46.3 0.9 copy.130
  47.2 1.2 copy_bitcast_fusion.8
  48.3 1.1 copy_bitcast_fusion.10
  49.5 1.5 slice_convert_fusion.8
  51.0 224.5 %all-gather.3.cloned.1.call-done = f32[1,100,16384]{2,0,1:T(1,128)} async-done(((f32[1,100,1024]{2,0,1:T(1,128)}), f32[1,100,16384]{2,0,1:T(1,128)}) %all-gather.3.cloned.1.call-update) | async-done | bytes 6553616 | tf_op jit(solution)/shard_map/all_gather | solution.py:56
  275.4 10.3 %copy.129 = f32[1,100,16384]{2,1,0:T(8,128)} copy(f32[1,100,16384]{2,0,1:T(1,128)} %all-gather.3.cloned.1.call-done) | data formatting | bytes 13107200
  285.8 6.9 %reshape.161 = bf16[240,16384]{1,0:T(8,128)(2,1)} reshape(bf16[16,15,16384]{2,1,0:T(8,128)(2,1)} %all-to-all-done.1) | data formatting | bytes 15728640 | tf_op jit(solution)/shard_map/reshape | solution.py:38
  292.7 12.6 %gather_fusion.1 = bf16[120,16384]{1,0:T(8,128)(2,1)} fusion(bf16[240,16384]{1,0:T(8,128)(2,1)} %reshape.161, s32[1024]{0:T(1024)S(1)} %pad_clamp_fusion), kind=kCustom, calls=%fused_computation.1 | custom fusion | bytes 7864800 | tf_op jit(solution)/shard_map/gather | solution.py:40
  305.4 6.5 %reshape.163 = f32[4,30,16384]{2,1,0:T(8,128)} reshape(bf16[120,16384]{1,0:T(8,128)(2,1)} %gather_fusion.1) | data formatting | bytes 11796480 | tf_op jit(solution)/shard_map/convert_element_type | solution.py:42
  311.9 21.0 %select_reduce_fusion.10 = (f32[4,16384]{1,0:T(4,128)S(1)}, f32[4,16384]{1,0:T(4,128)S(1)}, f32[4,16384]{1,0:T(4,128)S(1)}, f32[4,16384]{1,0:T(4,128)S(1)}, f32[...) fusion(f32[4,30,16384]{2,1,0:T(8,128)} %reshape.163, ...), kind=kLoop, calls=%fused_computation.22 | loop fusion | flops 58327040 | bytes 13107200 | tf_op jit(solution)/shard_map/reduce_sum | solution.py:17
  334.1 28.0 %select_reduce_fusion = f32[4,16384]{1,0:T(4,128)S(1)} fusion(f32[100,16384]{1,0:T(8,128)S(1)} %bitcast.168, s32[4,16384]{1,0:T(4,128)S(1)} %bitcast.180), kind=kLoop, calls=%fused_computation.2 | loop fusion | flops 19595264 | bytes 7077888 | tf_op jit(solution)/shard_map/reduce_sum | solution.py:17
  362.1 4.6 %psum.7 = f32[4]{0:T(128)S(1)} all-reduce(f32[4]{0:T(128)S(1)} %fusion.10), channel_id=1, replica_groups=mesh['day'=16,'tile'=2] {'tile'}, use_global_device_ids=true, to_apply=%region_13.14 | all-reduce | flops 4 | bytes 32 | tf_op jit(solution)/shard_map/psum | solution.py:52
  366.7 3.4 multiply_multiply_fusion
  370.2 22.2 %all_to_all.30 = f32[4,16,1024]{2,0,1:T(4,128)S(1)} all-to-all(f32[4,16,1024]{2,0,1:T(4,128)S(1)} %multiply_multiply_fusion), channel_id=1, replica_groups=mesh['day'=16,'tile'=2] {'day'}, dimensions={1} | all-to-all | bytes 524288 | tf_op jit(solution)/shard_map/all_to_all | solution.py:58
  (62 shorter events, 3.9 us)
Async XLA Ops:
  6.5 16.5 %copy-start = (bf16[32,1,16384]{2,0,1:T(8,128)(2,1)S(1)}, bf16[32,1,16384]{2,0,1:T(8,128)(2,1)}, u32[]{:S(2)}) copy-start(bf16[32,1,16384]{2,0,1:T(8,128)(2,1)} %param.9) | copy-start | bytes 3145732
  9.1 13.7 %all-to-all-start = ((s32[16,1,15]{2,1,0:T(1,128)}), s32[16,1,15]{2,1,0:T(1,128)S(1)}, u32[]{:S(2)}, u32[]{:S(2)}) async-start(s32[16,1,15]{2,1,0:T(1,128)} %bitcast.2), calls=%async_computation | async-start | bytes 16384 | tf_op jit(solution)/shard_map/all_to_all | solution.py:32
  15.6 259.8 %all-gather.3.cloned.1.call-start = ((), (), s32[]{:S(2)}) async-start(), calls=%async_computation.3 | async-start | bytes 6963200 | tf_op jit(solution)/shard_map/all_gather | solution.py:56
  38.5 6.5 %copy-start.10 = (s32[4,1,1,16384]{3,2,1,0:T(1,128)S(1)}, s32[4,1,1,16384]{3,2,1,0:T(1,128)}, u32[]{:S(2)}) copy-start(s32[4,1,1,16384]{3,2,1,0:T(1,128)} %get-tuple-element.18) | copy-start | bytes 786436
  38.5 6.5 %copy-start.11 = (s32[4,1,1,16384]{3,2,1,0:T(1,128)S(1)}, s32[4,1,1,16384]{3,2,1,0:T(1,128)}, u32[]{:S(2)}) copy-start(s32[4,1,1,16384]{3,2,1,0:T(1,128)} %get-tuple-element.19) | copy-start | bytes 786436
  38.5 7.7 %copy-start.17 = (s32[4,30]{1,0:T(4,128)S(1)}, s32[4,30]{1,0:T(4,128)}, u32[]{:S(2)}) copy-start(s32[4,30]{1,0:T(4,128)} %param.10) | copy-start | bytes 1444
  38.5 7.8 %copy-start.16 = (s32[4,1,16384]{2,1,0:T(1,128)S(1)}, s32[4,1,16384]{2,1,0:T(1,128)}, u32[]{:S(2)}) copy-start(s32[4,1,16384]{2,1,0:T(1,128)} %param.15) | copy-start | bytes 786436
  38.5 11.0 %copy-start.2 = (bf16[4,10,1,16384]{3,0,2,1:T(4,128)(2,1)S(1)}, bf16[4,10,1,16384]{3,0,2,1:T(4,128)(2,1)}, u32[]{:S(2)}) copy-start(bf16[4,10,1,16384]{3,0,2,1:T(4,128)(2,1)} %param.13) | copy-start | bytes 3932164
  38.5 247.3 %all-to-all-start.1 = ((bf16[16,15,16384]{2,1,0:T(8,128)(2,1)}), bf16[16,15,16384]{2,1,0:T(8,128)(2,1)}, u32[]{:S(2)}, u32[]{:S(2)}) async-start(bf16[16,15,16384]{2,1,0:T(8,128)(2,1)} %reshape.184), calls=%async_computation.1 | async-start | bytes 16777216 | tf_op jit(solution)/shard_map/all_to_all | solution.py:37
  305.3 6.5 %copy-start.12 = (s32[4,16384]{1,0:T(4,128)S(1)}, s32[4,16384]{1,0:T(4,128)}, u32[]{:S(2)}) copy-start(s32[4,16384]{1,0:T(4,128)} %get-tuple-element.35) | copy-start | bytes 786436
  305.3 6.5 %copy-start.13 = (s32[4,16384]{1,0:T(4,128)S(1)}, s32[4,16384]{1,0:T(4,128)}, u32[]{:S(2)}) copy-start(s32[4,16384]{1,0:T(4,128)} %get-tuple-element.36) | copy-start | bytes 786436
  305.3 6.5 %copy-start.14 = (s32[4,16384]{1,0:T(4,128)S(1)}, s32[4,16384]{1,0:T(4,128)}, u32[]{:S(2)}) copy-start(s32[4,16384]{1,0:T(4,128)} %get-tuple-element.37) | copy-start | bytes 786436
  305.3 6.5 %copy-start.15 = (s32[4,16384]{1,0:T(4,128)S(1)}, s32[4,16384]{1,0:T(4,128)}, u32[]{:S(2)}) copy-start(s32[4,16384]{1,0:T(4,128)} %get-tuple-element.38) | copy-start | bytes 786436
  311.9 22.2 %slice-start = ((s8[6815744]{0:T(1024)(128)(4,1)}), s8[4194304]{0:T(1024)(128)(4,1)S(1)}, s32[]{:S(2)}) async-start(s8[6815744]{0:T(1024)(128)(4,1)} %bitcast.166), calls=%async_computation.4 | async-start | bytes 8388608
  311.9 22.2 %slice-start.1 = ((s8[6815744]{0:T(1024)(128)(4,1)}), s8[2621440]{0:T(1024)(128)(4,1)S(1)}, s32[]{:S(2)}) async-start(s8[6815744]{0:T(1024)(128)(4,1)} %bitcast.166), calls=%async_computation.5 | async-start | bytes 5242880
  311.9 22.2 %copy-start.9 = (s32[4,1,16384]{2,0,1:T(4,128)S(1)}, s32[4,1,16384]{2,0,1:T(4,128)}, u32[]{:S(2)}) copy-start(s32[4,1,16384]{2,0,1:T(4,128)} %copy.130) | copy-start | bytes 786436
  332.9 0.9 copy-start.3
  333.0 0.9 copy-start.4
  333.0 0.9 copy-start.5
  333.0 0.9 copy-start.6
  333.0 1.0 copy-start.7
  333.0 1.1 copy-start.8
  333.0 33.7 %copy-start.18 = (f32[4]{0:T(128)S(1)}, f32[4]{0:T(128)}, u32[]{:S(2)}) copy-start(f32[4]{0:T(128)} %param.14) | copy-start | bytes 52
  333.0 60.1 %copy-start.1 = (bf16[32,1,16384]{2,0,1:T(8,128)(2,1)S(1)}, bf16[32,1,16384]{2,0,1:T(8,128)(2,1)}, u32[]{:S(2)}) copy-start(bf16[32,1,16384]{2,0,1:T(8,128)(2,1)} %param.9) | copy-start | bytes 3145732
Sparse Core Ops, SparseCore 0:
  19.1 256.2 all-gather.2
where the time goes:
time: 404 us; the launch traced here: 400 us
  waiting for transfers between devices  224 us (55%)
  local copies, waits for them, and re-layouts  64.7 us (16%)
  other arithmetic  57.4 us (14%)
  blocking collectives  26.8 us (7%)
  between operations  13.6 us (3%)
  starting transfers between devices  13 us (3%)
    all_gather x1, waiting for transfers between devices, per_device(): ratio = lax.all_gather(local_ratio, 'day', axis=1, tiled=True)  224 us
    reduce_sum x2, other arithmetic, lookup_rows(): return jnp.sum(jnp.where(hits, table, 0.0), axis=1)  49 us
    all_to_all x1, blocking collectives, per_device(): lax.all_to_all(value * factor, 'day', split_axis=1, concat_axis=0, tiled=...  22.2 us
    unnamed x49, local copies, waits for them, and re-layouts  17.3 us
    gather x2, local copies, waits for them, and re-layouts, per_device(): outgoing = library[:, 0, :][asked]  15.5 us
    gather x1, local copies, waits for them, and re-layouts, per_device(): received[slot_code].reshape(target_days, analog_owner.shape[1], cell_count)  12.6 us
  transfers between devices with their start and end apart: 3, of which 1 were waited for; matrix products, arithmetic and copies ran while one was open for 10% of the time, Pallas kernels for 0%

commit v1 on v0

v1 whole, which is shorter than its diff:
```python
import functools

import jax
import jax.numpy as jnp
from jax import lax
from jax.experimental import pallas as pl
from jax.experimental.pallas import tpu as pltpu
from jax.sharding import PartitionSpec as P

SLOTS = 32
HALVES = 2
LANES = 128


def pick_rows(read, groups, index):
    low = index & 7
    high = index >> 3
    out = jnp.take_along_axis(read(0), low, axis=0)
    for group in range(1, groups):
        part = jnp.take_along_axis(read(group), low, axis=0)
        out = jnp.where(high == group, part, out)
    return out


def kernel(
    sizes, lib, picks, weights, ranks, info, obs, hist, out,
    picks_in, weights_in, ranks_in, lib_recv, pw_send, pw_recv, rank_send, rank_recv,
    info_recv, rank_rows, prod, wts, comb, comb_in, sums_send, sums_recv, scale, table,
    local_sem, pick_sem, rank_sem, lib_ss, lib_rs, pw_ss, pw_rs, rk_ss, rk_rs,
    info_ss, info_rs, sum_ss, sum_rs, comb_ss, comb_rs,
):
    blocks, tiles, days, targets, analogs, cells = sizes
    group = blocks // HALVES
    total = blocks * tiles
    count = targets * analogs
    near = group * targets
    me = lax.axis_index("day")
    tile = lax.axis_index("tile")
    mine = me * tiles + tile
    half = me // group
    place = lax.rem(me, group)

    def columns(chunk):
        return pl.ds(pl.multiple_of(chunk * cells, LANES), cells)

    def pick_copy(r):
        return pltpu.make_async_copy(picks.at[r, 0], picks_in.at[r], pick_sem.at[r])

    def rank_copy(r):
        return pltpu.make_async_copy(ranks.at[r, 0], ranks_in.at[r], rank_sem.at[r])

    weight_copy = pltpu.make_async_copy(weights, weights_in, local_sem.at[0])
    weight_copy.start()
    lax.fori_loop(0, count, lambda r, c: (pick_copy(r).start(), c)[1], 0)
    for r in range(targets):
        rank_copy(r).start()

    barrier = pltpu.get_barrier_semaphore()

    def greet(j, c):
        peer = lax.rem(mine + j, total)
        pl.semaphore_signal(
            barrier, inc=1, device_id={"day": peer // tiles, "tile": lax.rem(peer, tiles)}
        )
        return c

    lax.fori_loop(1, total, greet, 0)
    pl.semaphore_wait(barrier, total - 1)

    def info_copy(src, peer):
        return pltpu.make_async_remote_copy(
            info, info_recv.at[src], info_ss.at[peer], info_rs.at[src], device_id={"day": peer}
        )

    def lib_copy(src, peer, m):
        return pltpu.make_async_remote_copy(
            lib.at[:, columns(lax.rem(peer, group) + group * m)],
            lib_recv.at[m, src],
            lib_ss.at[peer, m],
            lib_rs.at[src, m],
            device_id={"day": peer},
        )

    def own_copy(m):
        return pltpu.make_async_copy(
            lib.at[:, columns(place + group * m)], lib_recv.at[m, me], local_sem.at[1 + m]
        )

    def send_lib(j, c):
        peer = lax.rem(me + j, blocks)
        info_copy(me, peer).start()
        for m in range(HALVES):
            lib_copy(me, peer, m).start()
        return c

    for m in range(HALVES):
        own_copy(m).start()
    lax.fori_loop(1, blocks, send_lib, 0)
    info_recv[me] = info[...]

    def pw_copy(src, q):
        return pltpu.make_async_remote_copy(
            pw_send.at[q], pw_recv.at[src], pw_ss.at[q], pw_rs.at[src],
            device_id={"day": half * group + q},
        )

    def rank_out(src, peer):
        return pltpu.make_async_remote_copy(
            rank_send.at[peer], rank_recv.at[src], rk_ss.at[peer], rk_rs.at[src],
            device_id={"day": peer},
        )

    weight_copy.wait()
    lax.fori_loop(0, count, lambda r, c: (pick_copy(r).wait(), c)[1], 0)
    for r in range(targets):
        rank_copy(r).wait()

    def fill(q, dest):
        for m in range(HALVES):
            where = columns(q + group * m)
            for k in range(analogs):
                part = weights_in[k, :, where].astype(jnp.float32)
                for t in range(targets):
                    r = t * analogs + k
                    wts[r:r + 1, 0:cells] = part[t:t + 1]
            both = jnp.concatenate(
                [picks_in[:, where].astype(jnp.float32), wts[:, 0:cells]], axis=0
            )
            dest[:, m * cells:(m + 1) * cells] = both.astype(jnp.bfloat16)

    def send_pw(j, c):
        q = lax.rem(place + j, group)
        fill(q, pw_send.at[q])
        pw_copy(place, q).start()
        return c

    lax.fori_loop(1, group, send_pw, 0)
    fill(place, pw_recv.at[place])

    def send_rank(j, c):
        peer = lax.rem(me + j, blocks)
        rank_send[peer] = ranks_in[:, columns(peer)].astype(jnp.float32).astype(jnp.bfloat16)
        rank_out(me, peer).start()
        return c

    lax.fori_loop(1, blocks, send_rank, 0)
    rank_recv[me] = ranks_in[:, columns(me)].astype(jnp.float32).astype(jnp.bfloat16)

    bins = obs.shape[0]
    table[0:bins, :] = obs[...] / hist[...]
    if table.shape[0] > bins:
        table[bins:, :] = jnp.zeros((table.shape[0] - bins, cells), jnp.float32)

    def got_lib(j, c):
        src = lax.rem(me + blocks - j, blocks)
        info_copy(src, src).wait_recv()
        for m in range(HALVES):
            lib_copy(src, src, m).wait_recv()
        return c

    for m in range(HALVES):
        own_copy(m).wait()
    lax.fori_loop(1, blocks, got_lib, 0)

    day_ids = lax.broadcasted_iota(jnp.int32, (blocks * days, targets * SLOTS), 0)
    sub = lax.broadcasted_iota(jnp.int32, (8, cells), 0)

    def combine(s):
        wanted = info_recv[half * group + s][0:1, :].astype(jnp.int32)
        hot = (day_ids == wanted).astype(jnp.float32).astype(jnp.bfloat16)
        both = pw_recv[s].astype(jnp.float32)
        wts[...] = both[count:]
        for m in range(HALVES):
            fields = lax.dot_general(
                hot, lib_recv[m].reshape(blocks * days, cells),
                (((0,), (0,)), ((), ())), preferred_element_type=jnp.float32,
            )
            span = slice(m * cells, (m + 1) * cells)
            for v in range(count // 8):
                first = (8 * v) // analogs
                last = (8 * v + 7) // analogs
                rows = both[8 * v:8 * v + 8, span].astype(jnp.int32)

                def reader(t):
                    return lambda g: fields[t * SLOTS + 8 * g:t * SLOTS + 8 * g + 8]

                got = pick_rows(reader(first), SLOTS // 8, rows)
                for t in range(first + 1, last + 1):
                    more = pick_rows(reader(t), SLOTS // 8, rows)
                    got = jnp.where(sub + 8 * v >= t * analogs, more, got)
                here = slice(8 * v, 8 * v + 8)
                prod[here, span] = got * both[count + 8 * v:count + 8 * v + 8, span]
        for t in range(targets):
            here = slice(t * analogs, (t + 1) * analogs)
            top = jnp.sum(prod[here, :], axis=0, keepdims=True)
            bottom = jnp.sum(wts[here, :], axis=0, keepdims=True)
            row = top / bottom
            for m in range(HALVES):
                comb[m, pl.ds(s * targets + t, 1), :] = row[:, m * cells:(m + 1) * cells]

    combine(place)

    def arrive(j, c):
        s = lax.rem(place + group - j, group)
        pw_copy(s, s).wait_recv()
        combine(s)
        return c

    lax.fori_loop(1, group, arrive, 0)

    def comb_copy(src, dest):
        return pltpu.make_async_remote_copy(
            comb.at[dest], comb_in.at[src], comb_ss.at[dest], comb_rs.at[src],
            device_id={"day": dest * group + place},
        )

    for j in range(1, HALVES):
        comb_copy(half, lax.rem(half + j, HALVES)).start()

    width = min(near, LANES)
    square = (width, LANES)
    diagonal = lax.broadcasted_iota(jnp.int32, square, 0) == lax.broadcasted_iota(
        jnp.int32, square, 1
    )
    sums_send[...] = jnp.zeros(sums_send.shape, jnp.float32)
    for b in range(near // width):
        col = jnp.zeros((width, 1), jnp.float32)
        for m in range(HALVES):
            col += jnp.sum(comb[m, b * width:(b + 1) * width, :], axis=1, keepdims=True)
        sums_send[b:b + 1, :] = jnp.sum(
            jnp.where(diagonal, jnp.broadcast_to(col, square), 0.0), axis=0, keepdims=True
        )

    def sum_copy(src, peer):
        return pltpu.make_async_remote_copy(
            sums_send, sums_recv.at[src], sum_ss.at[peer], sum_rs.at[src],
            device_id={"day": peer // tiles, "tile": lax.rem(peer, tiles)},
        )

    lax.fori_loop(
        1, total, lambda j, c: (sum_copy(mine, lax.rem(mine + j, total)).start(), c)[1], 0
    )
    sums_recv[mine] = sums_send[...]

    def unpack(src):
        part = rank_recv[src].astype(jnp.float32).astype(jnp.int32)
        means = info_recv[src]
        for t in range(targets):
            rank_rows[pl.ds(src * targets + t, 1), :] = part[t:t + 1]
            scale[pl.ds(src * targets + t, 1), :] = means[4 + t:5 + t]

    unpack(me)

    def got_rank(j, c):
        src = lax.rem(me + blocks - j, blocks)
        rank_out(src, src).wait_recv()
        unpack(src)
        return c

    lax.fori_loop(1, blocks, got_rank, 0)
    lax.fori_loop(
        1, total,
        lambda j, c: (sum_copy(lax.rem(mine + total - j, total), 0).wait_recv(), c)[1], 0,
    )
    side = group * tiles
    for h in range(HALVES):
        acc = jnp.sum(sums_recv[h * side:(h + 1) * side], axis=0)
        for b in range(near // width):
            col = jnp.sum(
                jnp.where(diagonal, jnp.broadcast_to(acc[b:b + 1], square), 0.0),
                axis=1, keepdims=True,
            )
            here = slice(h * near + b * width, h * near + (b + 1) * width)
            scale[here, :] = scale[here, :] * float(cells * total) / col

    def finish(h, ref):
        def block(i, c):
            row = pl.multiple_of(h * near + 8 * i, 8)
            index = rank_rows[pl.ds(row, 8), :]
            factor = pick_rows(
                lambda g: table[8 * g:8 * g + 8, :], table.shape[0] // 8, index
            )
            value = ref[pl.ds(pl.multiple_of(8 * i, 8), 8), :] * scale[pl.ds(row, 8), :][:, 0:1]
            out[pl.ds(row, 8), :] = value * factor
            return c

        lax.fori_loop(0, near // 8, block, 0)

    finish(half, comb.at[half])
    for j in range(1, HALVES):
        src = lax.rem(half + j, HALVES)
        comb_copy(src, src).wait_recv()
        finish(src, comb_in.at[src])

    def drain(j, c):
        peer = lax.rem(me + j, blocks)
        info_copy(me, peer).wait_send()
        rank_out(me, peer).wait_send()
        for m in range(HALVES):
            lib_copy(me, peer, m).wait_send()
        return c

    lax.fori_loop(1, blocks, drain, 0)
    lax.fori_loop(
        1, group, lambda j, c: (pw_copy(place, lax.rem(place + j, group)).wait_send(), c)[1], 0
    )
    lax.fori_loop(
        1, total, lambda j, c: (sum_copy(mine, lax.rem(mine + j, total)).wait_send(), c)[1], 0
    )
    for j in range(1, HALVES):
        comb_copy(half, lax.rem(half + j, HALVES)).wait_send()


def per_device(
    library, analog_owner, analog_offset, picks, weights, target_mean, ranks, obs_quant, hist_quant
):
    blocks = lax.axis_size("day")
    tiles = lax.axis_size("tile")
    days = library.shape[0]
    targets, cands = analog_owner.shape
    analogs = picks.shape[1]
    cell_count = library.shape[2]
    cells = cell_count // blocks
    total_days = blocks * targets
    total = blocks * tiles
    group = blocks // HALVES
    near = group * targets
    count = targets * analogs
    bins = obs_quant.shape[1]
    padded = (bins + 7) // 8 * 8
    wide = HALVES * cells
    bf, f32, i32 = jnp.bfloat16, jnp.float32, jnp.int32

    day_list = (analog_owner * days + analog_offset).astype(f32)
    row = jnp.pad(day_list, ((0, 0), (0, SLOTS - cands))).reshape(1, targets * SLOTS)
    info = jnp.concatenate(
        [
            row,
            jnp.zeros((3, LANES), f32),
            jnp.broadcast_to(target_mean[:, None], (targets, LANES)),
        ],
        axis=0,
    )
    hbm = pl.BlockSpec(memory_space=pl.ANY)
    vmem = pl.BlockSpec(memory_space=pltpu.VMEM)
    dma = pltpu.SemaphoreType.DMA
    result = pl.pallas_call(
        functools.partial(kernel, (blocks, tiles, days, targets, analogs, cells)),
        out_shape=jax.ShapeDtypeStruct((total_days, cells), f32),
        in_specs=[hbm, hbm, hbm, hbm, vmem, vmem, vmem],
        out_specs=vmem,
        scratch_shapes=[
            pltpu.VMEM((count, cell_count), i32),
            pltpu.VMEM((analogs, targets, cell_count), bf),
            pltpu.VMEM((targets, cell_count), i32),
            pltpu.VMEM((HALVES, blocks, days, cells), bf),
            pltpu.VMEM((group, 2 * count, wide), bf),
            pltpu.VMEM((group, 2 * count, wide), bf),
            pltpu.VMEM((blocks, targets, cells), bf),
            pltpu.VMEM((blocks, targets, cells), bf),
            pltpu.VMEM((blocks, 8, LANES), f32),
            pltpu.VMEM((total_days, cells), i32),
            pltpu.VMEM((count, wide), f32),
            pltpu.VMEM((count, wide), f32),
            pltpu.VMEM((HALVES, near, cells), f32),
            pltpu.VMEM((HALVES, near, cells), f32),
            pltpu.VMEM((8, LANES), f32),
            pltpu.VMEM((total, 8, LANES), f32),
            pltpu.VMEM((total_days, LANES), f32),
            pltpu.VMEM((padded, cells), f32),
            dma((1 + HALVES,)),
            dma((count,)),
            dma((targets,)),
            dma((blocks, HALVES)),
            dma((blocks, HALVES)),
            dma((group,)),
            dma((group,)),
            dma((blocks,)),
            dma((blocks,)),
            dma((blocks,)),
            dma((blocks,)),
            dma((total,)),
            dma((total,)),
            dma((HALVES,)),
            dma((HALVES,)),
        ],
        compiler_params=pltpu.CompilerParams(
            collective_id=0, has_side_effects=True, vmem_limit_bytes=48 * 1024 * 1024
        ),
    )(
        library[:, 0],
        picks.reshape(count, 1, cell_count),
        weights[:, :, 0].transpose(1, 0, 2),
        ranks,
        info,
        obs_quant[0],
        hist_quant[0],
    )
    return result[None]


def solution(mesh):
    return jax.shard_map(
        per_device,
        mesh=mesh,
        in_specs=(
            P("day", "tile", None),
            P("day", None),
            P("day", None),
            P("day", None, "tile", None),
            P("day", None, "tile", None),
            P("day"),
            P("day", "tile", None),
            P("tile", None, "day"),
            P("tile", None, "day"),
        ),
        out_specs=P("tile", None, "day"),
        check_vma=False,
    )
```

time: 404 us -> 110 us (0.27)
  waiting for transfers between devices: 224 us -> 0 us
  Pallas kernels: 0 us -> 102 us
  local copies, waits for them, and re-layouts: 64.7 us -> 6.37 us
  other arithmetic: 57.4 us -> 0.78 us
  blocking collectives: 26.8 us -> 0 us
  between operations: 13.6 us -> 0.03 us
  starting transfers between devices: 13 us -> 0 us
    all_gather x1 -> x0, waiting for transfers between devices: 224 us -> none  [per_device(): ratio = lax.all_gather(local_ratio, 'day', axis=1, tiled=True)]
    pallas_call x0 -> x1, Pallas kernels: none -> 102 us  [per_device(): pl.pallas_call(functools.partial(kernel, (blocks, tiles, days, targets, a...]
    reduce_sum x5 -> x0, other arithmetic: 50.1 us -> none  [the longest x2 49 us: lookup_rows(): return jnp.sum(jnp.where(hits, table, 0.0), axis=1)]
    gather x3 -> x0, local copies, waits for them, and re-layouts: 28.1 us -> none  [the longest x2 15.5 us: per_device(): outgoing = library[:, 0, :][asked]]
    all_to_all x1 -> x0, blocking collectives: 22.2 us -> none  [per_device(): lax.all_to_all(value * factor, 'day', split_axis=1, concat_axis=0, tiled=...]
    all_to_all x2 -> x0, starting transfers between devices: 12.9 us -> none  [the longest x1 6.5 us: per_device(): lax.all_to_all(outgoing, 'day', split_axis=0, concat_axis=0, tiled=True)]
    unnamed x49 -> x8, local copies, waits for them, and re-layouts: 17.3 us -> 5.47 us
    reshape x2 -> x1, local copies, waits for them, and re-layouts: 7.79 us -> 0.09 us  [per_device(): jnp.pad(day_list, ((0, 0), (0, SLOTS - cands))).reshape(1, targets * SLOTS)]
  transfers between devices with their start and end apart: 3 -> 0, of which waited for: 1 -> 0; matrix products, arithmetic and copies ran while one was open for 10% -> 0% of each run, Pallas kernels for 0% -> 0%
where the time goes in v1:
time: 110 us
  Pallas kernels  102 us (93%)
  local copies, waits for them, and re-layouts  6.37 us (6%)
    pallas_call x1, Pallas kernels, per_device(): pl.pallas_call(functools.partial(kernel, (blocks, tiles, days, targets, a...  102 us
    unnamed x8, local copies, waits for them, and re-layouts  5.47 us

profile of v1, /device:TPU:25, one launch (start us, length us, event | category | flops | bytes accessed | tf_op | source)
XLA Modules:
  0.0 109.6 jit_solution(10209724120172280221)
XLA Ops:
  0.0 0.7 pad.7.clone
  0.7 0.1 pad.6.clone
  0.8 0.7 add_convert_fusion
  1.5 0.1 reshape.8
  1.6 0.1 maximum_maximum_fusion.info
  1.7 1.3 %copy_bitcast_fusion = (f32[100,1024]{1,0:T(8,128)S(1)}, f32[100,1024]{1,0:T(8,128)S(1)}) fusion(f32[1,100,1024]{2,0,1:T(1,128)} %param.17, f32[1,100,1024]{2,0,1:T(1,128)} %param.16), kind=kLoop, calls=%fused_computation | loop fusion | bytes 1638400
  3.0 0.0 copy-start
  3.0 1.3 %copy-done = bf16[4,10,1,16384]{3,0,2,1:T(4,128)(2,1)S(1)} copy-done((bf16[4,10,1,16384]{3,0,2,1:T(4,128)(2,1)S(1)}, bf16[4,10,1,16384]{3,0,2,1:T(4,128)(2,1)}, u32[]{:S(2)}) %copy-start) | copy-done | bytes 1310744
  4.3 0.0 copy-start.1
  4.3 1.2 %copy-done.1 = bf16[32,1,16384]{2,0,1:T(8,128)(2,1)S(1)} copy-done((bf16[32,1,16384]{2,0,1:T(8,128)(2,1)S(1)}, bf16[32,1,16384]{2,0,1:T(8,128)(2,1)}, u32[]{:S(2)}) %copy-start.1) | copy-done | bytes 1048600
  5.5 0.0 copy-start.2
  5.5 0.9 copy-done.2
  6.5 102.4 %shard_map.91 = f32[64,1024]{1,0:T(8,128)S(1)} custom-call(bf16[32,16384]{1,0:T(8,128)(2,1)S(1)} %bitcast.12, s32[40,1,16384]{2,1,0:T(1,128)} %bitcast.13, bf16[10,4,16384]{2,1,0:T(4,128)(2,1)S(1)} %bitcast.10, s32[4,1,16384]{2,1,0:T(1,128)S(1)} %copy-done.2, f32[8,128]{1,0:T(8,128)S(1)} %maximum_maximum_fusion.info, f32[100,1024]{1,0:T(8,128)S(1)} %get-tuple-element.6.obs, ...), custom_call_target="tpu_custom_call" | custom-call | tf_op jit(solution)/shard_map/pallas_call | solution.py:347
  108.9 0.7 copy.15
  (2 shorter events, 0.0 us)
Async XLA Ops:
  3.0 1.3 %copy-start = (bf16[4,10,1,16384]{3,0,2,1:T(4,128)(2,1)S(1)}, bf16[4,10,1,16384]{3,0,2,1:T(4,128)(2,1)}, u32[]{:S(2)}) copy-start(bf16[4,10,1,16384]{3,0,2,1:T(4,128)(2,1)} %param.13) | copy-start | bytes 3932164
  4.3 1.2 %copy-start.1 = (bf16[32,1,16384]{2,0,1:T(8,128)(2,1)S(1)}, bf16[32,1,16384]{2,0,1:T(8,128)(2,1)}, u32[]{:S(2)}) copy-start(bf16[32,1,16384]{2,0,1:T(8,128)(2,1)} %param.9) | copy-start | bytes 3145732
  5.5 0.9 copy-start.2

commit v2 on v1

--- a/solution.py
+++ b/solution.py
@@ -10,6 +10,8 @@
 SLOTS = 32
 HALVES = 2
 LANES = 128
+LEAD = 3
+PACE = 3
 
 
 def pick_rows(read, groups, index):
@@ -23,9 +25,10 @@
 
 
 def kernel(
-    sizes, lib, picks, weights, ranks, info, obs, hist, out,
+    sizes, lib, picks, weights, ranks, owner, offset, means_in, obs, hist, out,
     picks_in, weights_in, ranks_in, lib_recv, pw_send, pw_recv, rank_send, rank_recv,
     info_recv, rank_rows, prod, wts, comb, comb_in, sums_send, sums_recv, scale, table,
+    info, obs_in, hist_in, table_sem,
     local_sem, pick_sem, rank_sem, lib_ss, lib_rs, pw_ss, pw_rs, rk_ss, rk_rs,
     info_ss, info_rs, sum_ss, sum_rs, comb_ss, comb_rs,
 ):
@@ -86,21 +89,31 @@
             lib.at[:, columns(place + group * m)], lib_recv.at[m, me], local_sem.at[1 + m]
         )
 
-    def send_lib(j, c):
-        peer = lax.rem(me + j, blocks)
-        info_copy(me, peer).start()
-        for m in range(HALVES):
-            lib_copy(me, peer, m).start()
-        return c
-
+    def send_lib(i, c):
+        turn = i // (blocks - 1)
+        peer = lax.rem(me + 1 + lax.rem(i, blocks - 1), blocks)
+        lib_copy(me, peer, lax.rem(peer // group + 1 + turn, HALVES)).start()
+        return c
+
+    lax.fori_loop(0, LEAD, send_lib, 0)
     for m in range(HALVES):
         own_copy(m).start()
-    lax.fori_loop(1, blocks, send_lib, 0)
+    lists = owner[...] * days + offset[...]
+    info[...] = jnp.zeros(info.shape, jnp.float32)
+    for t in range(targets):
+        info[0:1, t * SLOTS:t * SLOTS + owner.shape[1]] = lists[t:t + 1].astype(jnp.float32)
+        info[4 + t:5 + t, :] = jnp.broadcast_to(means_in[0:1, t:t + 1], (1, LANES))
     info_recv[me] = info[...]
 
-    def pw_copy(src, q):
-        return pltpu.make_async_remote_copy(
-            pw_send.at[q], pw_recv.at[src], pw_ss.at[q], pw_rs.at[src],
+    def send_info(j, c):
+        info_copy(me, lax.rem(me + j, blocks)).start()
+        return c
+
+    lax.fori_loop(1, blocks, send_info, 0)
+
+    def pw_copy(src, q, m):
+        return pltpu.make_async_remote_copy(
+            pw_send.at[m, q], pw_recv.at[m, src], pw_ss.at[m, q], pw_rs.at[m, src],
             device_id={"day": half * group + q},
         )
 
@@ -115,27 +128,37 @@
     for r in range(targets):
         rank_copy(r).wait()
 
-    def fill(q, dest):
-        for m in range(HALVES):
-            where = columns(q + group * m)
-            for k in range(analogs):
-                part = weights_in[k, :, where].astype(jnp.float32)
-                for t in range(targets):
-                    r = t * analogs + k
-                    wts[r:r + 1, 0:cells] = part[t:t + 1]
-            both = jnp.concatenate(
-                [picks_in[:, where].astype(jnp.float32), wts[:, 0:cells]], axis=0
-            )
-            dest[:, m * cells:(m + 1) * cells] = both.astype(jnp.bfloat16)
-
-    def send_pw(j, c):
-        q = lax.rem(place + j, group)
-        fill(q, pw_send.at[q])
-        pw_copy(place, q).start()
-        return c
-
-    lax.fori_loop(1, group, send_pw, 0)
-    fill(place, pw_recv.at[place])
+    def fill(q, m, dest):
+        where = columns(q + group * m)
+        for k in range(analogs):
+            part = weights_in[k, :, where].astype(jnp.float32)
+            for t in range(targets):
+                r = t * analogs + k
+                wts[r:r + 1, :] = part[t:t + 1]
+        both = jnp.concatenate([picks_in[:, where].astype(jnp.float32), wts[...]], axis=0)
+        dest[...] = both.astype(jnp.bfloat16)
+
+    def turn_of(turn):
+        return lax.rem(half + 1 + turn, HALVES)
+
+    def send_pw(i, c):
+        m = turn_of(i // (group - 1))
+        q = lax.rem(place + 1 + lax.rem(i, group - 1), group)
+        fill(q, m, pw_send.at[m, q])
+        pw_copy(place, q, m).start()
+        last = HALVES * (blocks - 1)
+        lax.fori_loop(
+            jnp.minimum(LEAD + PACE * i, last), jnp.minimum(LEAD + PACE * (i + 1), last), send_lib, 0
+        )
+        return c
+
+    steps = HALVES * (group - 1)
+    lax.fori_loop(0, steps, send_pw, 0)
+    lax.fori_loop(
+        min(LEAD + PACE * steps, HALVES * (blocks - 1)), HALVES * (blocks - 1), send_lib, 0
+    )
+    for m in range(HALVES):
+        fill(place, m, pw_recv.at[m, place])
 
     def send_rank(j, c):
         peer = lax.rem(me + j, blocks)
@@ -147,66 +170,56 @@
     rank_recv[me] = ranks_in[:, columns(me)].astype(jnp.float32).astype(jnp.bfloat16)
 
     bins = obs.shape[0]
-    table[0:bins, :] = obs[...] / hist[...]
+
+    def table_copies(r):
+        return (
+            pltpu.make_async_copy(obs.at[r, 0], obs_in.at[r], table_sem.at[0, r]),
+            pltpu.make_async_copy(hist.at[r, 0], hist_in.at[r], table_sem.at[1, r]),
+        )
+
+    lax.fori_loop(0, bins, lambda r, c: ([x.start() for x in table_copies(r)], c)[1], 0)
+    lax.fori_loop(0, bins, lambda r, c: ([x.wait() for x in table_copies(r)], c)[1], 0)
+    table[0:bins, :] = obs_in[...] / hist_in[...]
     if table.shape[0] > bins:
         table[bins:, :] = jnp.zeros((table.shape[0] - bins, cells), jnp.float32)
 
-    def got_lib(j, c):
+    def got_info(j, c):
         src = lax.rem(me + blocks - j, blocks)
         info_copy(src, src).wait_recv()
-        for m in range(HALVES):
-            lib_copy(src, src, m).wait_recv()
-        return c
-
-    for m in range(HALVES):
-        own_copy(m).wait()
-    lax.fori_loop(1, blocks, got_lib, 0)
-
+        return c
+
+    lax.fori_loop(1, blocks, got_info, 0)
     day_ids = lax.broadcasted_iota(jnp.int32, (blocks * days, targets * SLOTS), 0)
     sub = lax.broadcasted_iota(jnp.int32, (8, cells), 0)
 
-    def combine(s):
+    def combine(s, m):
         wanted = info_recv[half * group + s][0:1, :].astype(jnp.int32)
         hot = (day_ids == wanted).astype(jnp.float32).astype(jnp.bfloat16)
-        both = pw_recv[s].astype(jnp.float32)
+        both = pw_recv[m, s].astype(jnp.float32)
         wts[...] = both[count:]
-        for m in range(HALVES):
-            fields = lax.dot_general(
-                hot, lib_recv[m].reshape(blocks * days, cells),
-                (((0,), (0,)), ((), ())), preferred_element_type=jnp.float32,
-            )
-            span = slice(m * cells, (m + 1) * cells)
-            for v in range(count // 8):
-                first = (8 * v) // analogs
-                last = (8 * v + 7) // analogs
-                rows = both[8 * v:8 * v + 8, span].astype(jnp.int32)
-
-                def reader(t):
-                    return lambda g: fields[t * SLOTS + 8 * g:t * SLOTS + 8 * g + 8]
-
-                got = pick_rows(reader(first), SLOTS // 8, rows)
-                for t in range(first + 1, last + 1):
-                    more = pick_rows(reader(t), SLOTS // 8, rows)
-                    got = jnp.where(sub + 8 * v >= t * analogs, more, got)
-                here = slice(8 * v, 8 * v + 8)
-                prod[here, span] = got * both[count + 8 * v:count + 8 * v + 8, span]
+        fields = lax.dot_general(
+            hot, lib_recv[m].reshape(blocks * days, cells),
+            (((0,), (0,)), ((), ())), preferred_element_type=jnp.float32,
+        )
+        for v in range(count // 8):
+            first = (8 * v) // analogs
+            last = (8 * v + 7) // analogs
+            here = slice(8 * v, 8 * v + 8)
+            rows = both[here].astype(jnp.int32)
+
+            def reader(t):
+                return lambda g: fields[t * SLOTS + 8 * g:t * SLOTS + 8 * g + 8]
+
+            got = pick_rows(reader(first), SLOTS // 8, rows)
+            for t in range(first + 1, last + 1):
+                more = pick_rows(reader(t), SLOTS // 8, rows)
+                got = jnp.where(sub + 8 * v >= t * analogs, more, got)
+            prod[here, :] = got * both[count + 8 * v:count + 8 * v + 8]
         for t in range(targets):
             here = slice(t * analogs, (t + 1) * analogs)
             top = jnp.sum(prod[here, :], axis=0, keepdims=True)
             bottom = jnp.sum(wts[here, :], axis=0, keepdims=True)
-            row = top / bottom
-            for m in range(HALVES):
-                comb[m, pl.ds(s * targets + t, 1), :] = row[:, m * cells:(m + 1) * cells]
-
-    combine(place)
-
-    def arrive(j, c):
-        s = lax.rem(place + group - j, group)
-        pw_copy(s, s).wait_recv()
-        combine(s)
-        return c
-
-    lax.fori_loop(1, group, arrive, 0)
+            comb[m, pl.ds(s * targets + t, 1), :] = top / bottom
 
     def comb_copy(src, dest):
         return pltpu.make_async_remote_copy(
@@ -214,8 +227,26 @@
             device_id={"day": dest * group + place},
         )
 
-    for j in range(1, HALVES):
-        comb_copy(half, lax.rem(half + j, HALVES)).start()
+    for turn in range(HALVES):
+        m = turn_of(turn)
+
+        def got_lib(j, c):
+            src = lax.rem(me + blocks - j, blocks)
+            lib_copy(src, src, m).wait_recv()
+            return c
+
+        def arrive(j, c):
+            s = lax.rem(place + group - j, group)
+            pw_copy(s, s, m).wait_recv()
+            combine(s, m)
+            return c
+
+        own_copy(m).wait()
+        lax.fori_loop(1, blocks, got_lib, 0)
+        combine(place, m)
+        lax.fori_loop(1, group, arrive, 0)
+        if turn < HALVES - 1:
+            comb_copy(half, m).start()
 
     width = min(near, LANES)
     square = (width, LANES)
@@ -301,9 +332,11 @@
         return c
 
     lax.fori_loop(1, blocks, drain, 0)
-    lax.fori_loop(
-        1, group, lambda j, c: (pw_copy(place, lax.rem(place + j, group)).wait_send(), c)[1], 0
-    )
+    for m in range(HALVES):
+        lax.fori_loop(
+            1, group,
+            lambda j, c: (pw_copy(place, lax.rem(place + j, group), m).wait_send(), c)[1], 0,
+        )
     lax.fori_loop(
         1, total, lambda j, c: (sum_copy(mine, lax.rem(mine + j, total)).wait_send(), c)[1], 0
     )
@@ -317,7 +350,7 @@
     blocks = lax.axis_size("day")
     tiles = lax.axis_size("tile")
     days = library.shape[0]
-    targets, cands = analog_owner.shape
+    targets = analog_owner.shape[0]
     analogs = picks.shape[1]
     cell_count = library.shape[2]
     cells = cell_count // blocks
@@ -328,53 +361,46 @@
     count = targets * analogs
     bins = obs_quant.shape[1]
     padded = (bins + 7) // 8 * 8
-    wide = HALVES * cells
     bf, f32, i32 = jnp.bfloat16, jnp.float32, jnp.int32
 
-    day_list = (analog_owner * days + analog_offset).astype(f32)
-    row = jnp.pad(day_list, ((0, 0), (0, SLOTS - cands))).reshape(1, targets * SLOTS)
-    info = jnp.concatenate(
-        [
-            row,
-            jnp.zeros((3, LANES), f32),
-            jnp.broadcast_to(target_mean[:, None], (targets, LANES)),
-        ],
-        axis=0,
-    )
     hbm = pl.BlockSpec(memory_space=pl.ANY)
     vmem = pl.BlockSpec(memory_space=pltpu.VMEM)
     dma = pltpu.SemaphoreType.DMA
     result = pl.pallas_call(
         functools.partial(kernel, (blocks, tiles, days, targets, analogs, cells)),
         out_shape=jax.ShapeDtypeStruct((total_days, cells), f32),
-        in_specs=[hbm, hbm, hbm, hbm, vmem, vmem, vmem],
+        in_specs=[hbm, hbm, hbm, hbm, vmem, vmem, vmem, hbm, hbm],
         out_specs=vmem,
         scratch_shapes=[
             pltpu.VMEM((count, cell_count), i32),
             pltpu.VMEM((analogs, targets, cell_count), bf),
             pltpu.VMEM((targets, cell_count), i32),
             pltpu.VMEM((HALVES, blocks, days, cells), bf),
-            pltpu.VMEM((group, 2 * count, wide), bf),
-            pltpu.VMEM((group, 2 * count, wide), bf),
+            pltpu.VMEM((HALVES, group, 2 * count, cells), bf),
+            pltpu.VMEM((HALVES, group, 2 * count, cells), bf),
             pltpu.VMEM((blocks, targets, cells), bf),
             pltpu.VMEM((blocks, targets, cells), bf),
             pltpu.VMEM((blocks, 8, LANES), f32),
             pltpu.VMEM((total_days, cells), i32),
-            pltpu.VMEM((count, wide), f32),
-            pltpu.VMEM((count, wide), f32),
+            pltpu.VMEM((count, cells), f32),
+            pltpu.VMEM((count, cells), f32),
             pltpu.VMEM((HALVES, near, cells), f32),
             pltpu.VMEM((HALVES, near, cells), f32),
             pltpu.VMEM((8, LANES), f32),
             pltpu.VMEM((total, 8, LANES), f32),
             pltpu.VMEM((total_days, LANES), f32),
             pltpu.VMEM((padded, cells), f32),
+            pltpu.VMEM((8, LANES), f32),
+            pltpu.VMEM((bins, cells), f32),
+            pltpu.VMEM((bins, cells), f32),
+            dma((2, bins)),
             dma((1 + HALVES,)),
             dma((count,)),
             dma((targets,)),
             dma((blocks, HALVES)),
             dma((blocks, HALVES)),
-            dma((group,)),
-            dma((group,)),
+            dma((HALVES, group)),
+            dma((HALVES, group)),
             dma((blocks,)),
             dma((blocks,)),
             dma((blocks,)),
@@ -385,16 +411,18 @@
             dma((HALVES,)),
         ],
         compiler_params=pltpu.CompilerParams(
-            collective_id=0, has_side_effects=True, vmem_limit_bytes=48 * 1024 * 1024
+            collective_id=0, has_side_effects=True, vmem_limit_bytes=60 * 1024 * 1024
         ),
     )(
         library[:, 0],
         picks.reshape(count, 1, cell_count),
         weights[:, :, 0].transpose(1, 0, 2),
         ranks,
-        info,
-        obs_quant[0],
-        hist_quant[0],
+        analog_owner,
+        analog_offset,
+        target_mean.reshape(1, targets),
+        obs_quant.reshape(bins, 1, cells),
+        hist_quant.reshape(bins, 1, cells),
     )
     return result[None]
 

time: 110 us -> 96.6 us (0.88)
  Pallas kernels: 102 us -> 93.6 us
  local copies, waits for them, and re-layouts: 6.37 us -> 1.67 us
    pallas_call x1, Pallas kernels: 102 us -> 93.6 us  [per_device(): pl.pallas_call(functools.partial(kernel, (blocks, tiles, days, targets, a...]
    unnamed x8 -> x1, local copies, waits for them, and re-layouts: 5.47 us -> 1.67 us
where the time goes in v2:
time: 96.6 us; the launch traced here: 95.2 us
  Pallas kernels  93.6 us (97%)
  local copies, waits for them, and re-layouts  1.67 us (2%)
    pallas_call x1, Pallas kernels, per_device(): pl.pallas_call(functools.partial(kernel, (blocks, tiles, days, targets, a...  93.6 us

profile of v2, /device:TPU:25, one launch (start us, length us, event | category | flops | bytes accessed | tf_op | source)
XLA Modules:
  0.0 95.2 jit_solution(3528970682993939512)
XLA Ops:
  0.0 93.6 %shard_map.91 = f32[64,1024]{1,0:T(8,128)} custom-call(bf16[32,16384]{1,0:T(8,128)(2,1)} %bitcast.12, s32[40,1,16384]{2,1,0:T(1,128)} %bitcast.9, bf16[10,4,16384]{2,1,0:T(4,128)(2,1)} %bitcast.10, s32[4,1,16384]{2,1,0:T(1,128)} %ranks.1, s32[4,30]{1,0:T(4,128)} %owner.1, s32[4,30]{1,0:T(4,128)} %offset.1, f32[1,4]{1,0:T(1,128)} %bitcast.15, ...), custom_call_target="tpu_custom_call" | custom-call | tf_op jit(solution)/shard_map/pallas_call | solution.py:369
  93.6 1.7 %copy.11 = f32[1,64,1024]{2,1,0:T(8,128)} copy(f32[1,64,1024]{2,1,0:T(8,128)} %bitcast.11) | data formatting | bytes 524288

commit v3 on v2

--- a/solution.py
+++ b/solution.py
@@ -91,7 +91,8 @@
 
     def send_lib(i, c):
         turn = i // (blocks - 1)
-        peer = lax.rem(me + 1 + lax.rem(i, blocks - 1), blocks)
+        away = 1 + lax.rem(i, blocks - 1)
+        peer = lax.rem(me + away + tile * (blocks - 2 * away), blocks)
         lib_copy(me, peer, lax.rem(peer // group + 1 + turn, HALVES)).start()
         return c
 
@@ -143,7 +144,8 @@
 
     def send_pw(i, c):
         m = turn_of(i // (group - 1))
-        q = lax.rem(place + 1 + lax.rem(i, group - 1), group)
+        away = 1 + lax.rem(i, group - 1)
+        q = lax.rem(place + away + tile * (group - 2 * away), group)
         fill(q, m, pw_send.at[m, q])
         pw_copy(place, q, m).start()
         last = HALVES * (blocks - 1)

time: 96.6 us -> 92.5 us (0.958)
  Pallas kernels: 93.6 us -> 89.3 us
    pallas_call x1, Pallas kernels: 93.6 us -> 89.3 us  [per_device(): pl.pallas_call(functools.partial(kernel, (blocks, tiles, days, targets, a...]
where the time goes in v3:
time: 92.5 us; the launch traced here: 91 us
  Pallas kernels  89.3 us (97%)
  local copies, waits for them, and re-layouts  1.67 us (2%)
    pallas_call x1, Pallas kernels, per_device(): pl.pallas_call(functools.partial(kernel, (blocks, tiles, days, targets, a...  89.3 us

profile of v3, /device:TPU:25, one launch (start us, length us, event | category | flops | bytes accessed | tf_op | source)
XLA Modules:
  0.0 91.0 jit_solution(7228296728028272370)
XLA Ops:
  0.0 89.3 %shard_map.91 = f32[64,1024]{1,0:T(8,128)} custom-call(bf16[32,16384]{1,0:T(8,128)(2,1)} %bitcast.12, s32[40,1,16384]{2,1,0:T(1,128)} %bitcast.9, bf16[10,4,16384]{2,1,0:T(4,128)(2,1)} %bitcast.10, s32[4,1,16384]{2,1,0:T(1,128)} %ranks.1, s32[4,30]{1,0:T(4,128)} %owner.1, s32[4,30]{1,0:T(4,128)} %offset.1, f32[1,4]{1,0:T(1,128)} %bitcast.15, ...), custom_call_target="tpu_custom_call" | custom-call | tf_op jit(solution)/shard_map/pallas_call | solution.py:371
  89.3 1.7 %copy.11 = f32[1,64,1024]{2,1,0:T(8,128)} copy(f32[1,64,1024]{2,1,0:T(8,128)} %bitcast.11) | data formatting | bytes 524288
